TPU v7x, 32 devices: a whole 2x2x4 slice. The times are simulated.
32 devices in a mesh: groups: 2 (over x), lon: 16 (over z, y, core).
Axes of the slice: x: 2, y: 2, z: 4, core: 2. Of those that a mesh axis runs over, the one named last changes fastest.
Arguments:
- state_in: bfloat16 [128, 768, 256], P('groups', 'lon'), parts along dimension 0, may hold values from -6 to 6
- target: bfloat16 [128, 768, 256], P('groups', 'lon'), parts along dimension 0, may hold values from -6 to 6
- ocean_mask: int32 [128, 768], P('groups', 'lon'), parts along dimension 0, may hold values from 0 to 1, as said below
- kernel_one: bfloat16 [3, 3, 256, 256], replicated, may hold values from -0.125 to 0.125
- kernel_two: bfloat16 [3, 3, 256, 256], replicated, may hold values from -0.125 to 0.125
Outputs:
- prediction: bfloat16 [128, 768, 256], P('groups', 'lon'), parts along dimension 0
- grad_one: float32 [6, 3, 256, 256], P('groups'), parts along dimension 0
- grad_two: float32 [6, 3, 256, 256], P('groups'), parts along dimension 0
There are 2 independent parts, one for each index of `groups`. A program takes and returns all parts, laid end to end along the dimension named above; an argument that names none is the same for every part. Nothing has to cross between parts.
Inputs may be any that keep to these rules, and one draw needn't show every extreme that they name: `ocean_mask`: 1 marks an ocean cell and 0 a land cell.
All inputs are finite; a program needn't handle non-finite values.
Results may differ from a plain program's by a relative error of at most 0.02.
Values may be sent and summed in bfloat16 or wider, within the bound.
A program may use at most 192 MiB of HBM per device.

v0:
```python
import math

import jax
import jax.numpy as jnp
from jax import lax
from jax.sharding import PartitionSpec as P


def from_partner(shard, axis, distance):
    return lax.ppermute(shard, axis, [(i, i ^ 1 << distance) for i in range(lax.axis_size(axis))])


def padded_2(block, sides, width):
    for axis, dim in sides:
        count = lax.axis_size(axis)
        forward = [(i, i + 1) for i in range(count - 1)]
        forward.append((count - 1, 0))
        backward = [(target, source) for source, target in forward]
        low = lax.ppermute(
            lax.slice_in_dim(block, block.shape[dim] - width, None, axis=dim), axis, forward
        )
        high = lax.ppermute(lax.slice_in_dim(block, 0, width, axis=dim), axis, backward)
        block = jnp.concatenate([low, block, high], axis=dim)
    return block


def mirror_row(edge_row):
    bit_count = lax.axis_size("lon").bit_length() - 1
    bit_order = list(range(bit_count))
    picked = edge_row
    for which_bit in bit_order:
        picked = from_partner(picked, "lon", which_bit)
    return picked[:, ::-1]


def extend(values_in):
    wide = padded_2(values_in, (("lon", 1),), 1)
    north = mirror_row(wide[-1:])
    return (wide, north)


def padded_field(values_in):
    wide, north = extend(values_in)
    blank_row = jnp.zeros_like(wide[:1])
    return jnp.concatenate([blank_row, wide, north], axis=0)


def patches(padded, height, width):
    pieces = [padded[a : a + height, b : b + width] for a in range(3) for b in range(3)]
    return jnp.concatenate(pieces, axis=2).reshape(height * width, 9 * padded.shape[2])


def gelu_value(u):
    return u * 0.5 * (1.0 + jax.scipy.special.erf(u / math.sqrt(2.0)))


def gelu_slope(u):
    return 0.5 * (1.0 + jax.scipy.special.erf(u / math.sqrt(2.0))) + u * jnp.exp(
        -0.5 * u * u
    ) / math.sqrt(2.0 * math.pi)


def kernel_terms(patch_rows, error_rows):
    return lax.dot_general(
        patch_rows, error_rows, (((0,), (0,)), ((), ())), preferred_element_type=jnp.float32
    )


def local(state_in, target, ocean_mask, kernel_one, kernel_two):
    height, width, channels = state_in.shape
    is_ocean = ocean_mask[..., None] == 1
    oceanic = ocean_mask[..., None].astype(jnp.float32)
    masked = jnp.where(is_ocean, state_in, jnp.zeros_like(state_in))
    patches_one = patches(padded_field(masked), height, width)
    pre_flat = jnp.dot(
        patches_one, kernel_one.reshape(9 * channels, channels), preferred_element_type=jnp.float32
    )
    pre_act = pre_flat.reshape(height, width, channels).astype(jnp.bfloat16)
    pre_value = pre_act.astype(jnp.float32)
    hidden = (gelu_value(pre_value) * oceanic).astype(jnp.bfloat16)
    patches_two = patches(padded_field(hidden), height, width)
    output = jnp.dot(
        patches_two, kernel_two.reshape(9 * channels, channels), preferred_element_type=jnp.float32
    )
    output = output.reshape(height, width, channels)
    prediction = (output * oceanic).astype(jnp.bfloat16)
    error_scale = 1.0 / math.sqrt(height * width * lax.axis_size("lon"))
    error_map = (oceanic * (output - target.astype(jnp.float32)) * error_scale).astype(jnp.bfloat16)
    error_rows = error_map.reshape(height * width, channels)
    terms_two = kernel_terms(patches_two, error_rows).reshape(3, 3, channels, channels)
    error_wide, error_north = extend(error_map)
    blank_row = jnp.zeros_like(error_wide[:1])
    error_pad = jnp.concatenate([blank_row, error_wide, blank_row], axis=0)
    pieces = [
        error_pad[2 - a : 2 - a + height, 2 - b : 2 - b + width] for a in range(3) for b in range(3)
    ]
    stacked = jnp.stack(pieces, axis=2).reshape(height * width, 9, channels)
    kernel_nine = kernel_two.reshape(9, channels, channels)
    hidden_grad = lax.dot_general(
        stacked, kernel_nine, (((1, 2), (0, 2)), ((), ())), preferred_element_type=jnp.float32
    )
    hidden_grad = hidden_grad.reshape(height, width, channels)
    north_rows = jnp.stack([error_north[0, b : b + width] for b in range(3)], axis=1)
    fold_term = lax.dot_general(
        north_rows, kernel_two[2], (((1, 2), (0, 2)), ((), ())), preferred_element_type=jnp.float32
    )
    hidden_grad = hidden_grad.at[height - 1].add(fold_term)
    pre_grad = (hidden_grad * gelu_slope(pre_value) * oceanic).astype(jnp.bfloat16)
    terms_one = kernel_terms(patches_one, pre_grad.reshape(height * width, channels)).reshape(
        3, 3, channels, channels
    )
    grad_one, grad_two = (
        lax.psum(terms_one.astype(jnp.bfloat16), "lon").astype(jnp.float32),
        lax.psum(terms_two.astype(jnp.bfloat16), "lon").astype(jnp.float32),
    )
    return (prediction, grad_one, grad_two)


def solution(mesh):
    return jax.shard_map(
        local,
        mesh=mesh,
        in_specs=(P("groups", "lon", None), P("groups", "lon", None), P("groups", "lon"), P(), P()),
        out_specs=(
            P("groups", "lon", None),
            P("groups", None, None, None),
            P("groups", None, None, None),
        ),
        check_vma=False,
    )
```

profile of v0, /device:TPU:0, one launch (start us, length us, event | category | flops | bytes accessed | tf_op | source)
XLA Modules:
  0.0 292.8 jit_solution(4038720375554322817)
XLA Ops:
  10.5 5.1 %collective-permute-start.1 = (bf16[64,1,256]{2,1,0:T(2,128)(2,1)S(1)}, bf16[64,1,256]{2,1,0:T(2,128)(2,1)S(1)}, u32[]{:S(2)}, u32[]{:S(2)}) collective-permute-start(bf16[64,1,256]{2,1,0:T(2,128)(2,1)S(1)} %get-tuple-element.24), channel_id=1, source_target_pairs={{1,0},{2,1},{3,2},{4,3},{5,4},{6,5},{7,6},{8,7},{9,8},{10,9},{11,1... | collective-permute-start | bytes 98312 | tf_op jit(solution)/shard_map/ppermute | solution.py:22
  15.7 1.9 collective-permute-done
  20.0 2.2 slice_dynamic-update-slice_fusion.10
  22.3 2.2 slice_dynamic-update-slice_fusion.9
  26.2 2.1 fusion.18
  32.2 2.5 collective-permute-start.5
  34.8 2.3 fusion.17
  39.7 2.1 slice_dynamic-update-slice_fusion.4
  41.8 2.1 slice_dynamic-update-slice_fusion.3
  43.9 8.1 %fusion.2 = (bf16[64,48,256]{2,1,0:T(8,128)(2,1)S(1)}, bf16[64,48,256]{2,1,0:T(8,128)(2,1)}) fusion(f32[64,48]{1,0:T(8,128)S(1)} %copy.9, bf16[64,48,2304]{2,1,0:T(8,128)(2,1)} %slice_dynamic-update-slice_fusion.3, bf16[2304,256,1]{1,0,2:T(8,128)(2,1)S(1)} %bitcast.80), kind=kOutput, calls=%fused_computation.7 | convolution fusion | flops 3630170112 | bytes 18493440 | tf_op jit(solution)/shard_map/dot_general | solution.py:75
  52.1 4.7 %collective-permute-start.7 = (bf16[64,1,256]{2,1,0:T(2,128)(2,1)S(1)}, bf16[64,1,256]{2,1,0:T(2,128)(2,1)S(1)}, u32[]{:S(2)}, u32[]{:S(2)}) collective-permute-start(bf16[64,1,256]{2,1,0:T(2,128)(2,1)S(1)} %get-tuple-element.22), channel_id=1, source_target_pairs={{1,0},{2,1},{3,2},{4,3},{5,4},{6,5},{7,6},{8,7},{9,8},{10,9},{11,1... | collective-permute-start | bytes 98312 | tf_op jit(solution)/shard_map/ppermute | solution.py:22
  56.8 18.6 %copy.10 = bf16[2304,3072]{1,0:T(8,128)(2,1)} copy(bf16[2304,3072]{0,1:T(8,128)(2,1)} %bitcast.5) | data formatting | bytes 28311552 | tf_op jit(solution)/shard_map/dot_general | solution.py:64
  77.9 2.2 slice_dynamic-update-slice_fusion.7
  80.1 2.2 slice_dynamic-update-slice_fusion.6
  82.3 2.1 fusion.16
  87.6 2.4 collective-permute-done.10
  90.8 2.3 fusion.15
  93.1 1.8 collective-permute-done.11
  97.4 2.1 slice_dynamic-update-slice_fusion.1
  99.6 2.1 slice_dynamic-update-slice_fusion
  101.7 18.8 %copy.12 = bf16[2304,3072]{1,0:T(8,128)(2,1)} copy(bf16[2304,3072]{0,1:T(8,128)(2,1)} %bitcast.30) | data formatting | bytes 28311552 | tf_op jit(solution)/shard_map/dot_general | solution.py:64
  120.5 10.3 %multiply_convert_fusion = (bf16[64,48,256]{2,1,0:T(8,128)(2,1)S(1)}, bf16[64,48,256]{2,1,0:T(8,128)(2,1)}) fusion(bf16[64,48,256]{2,1,0:T(8,128)(2,1)S(1)} %copy-done.7, f32[64,48]{1,0:T(8,128)S(1)} %copy.9, bf16[64,48,2304]{2,1,0:T(8,128)(2,1)} %slice_dynamic-update-slice_fusion, bf16[2304,256,1]{1,0,2:T(8,128)(2,1)S(1)} %bitcast.88), kind=kOutput, calls=%fused_computation.16 | convolution fusion | flops 3629383680 | bytes 20066304 | tf_op jit(solution)/shard_map/dot_general | solution.py:82
  131.0 12.9 %collective-permute-start.13 = (bf16[64,1,256]{2,1,0:T(2,128)(2,1)S(1)}, bf16[64,1,256]{2,1,0:T(2,128)(2,1)S(1)}, u32[]{:S(2)}, u32[]{:S(2)}) collective-permute-start(bf16[64,1,256]{2,1,0:T(2,128)(2,1)S(1)} %get-tuple-element.20), channel_id=1, source_target_pairs={{1,0},{2,1},{3,2},{4,3},{5,4},{6,5},{7,6},{8,7},{9,8},{10,9},{11,1... | collective-permute-start | bytes 98312 | tf_op jit(solution)/shard_map/ppermute | solution.py:22
  143.9 4.9 %convolution_convert_fusion.1 = bf16[3,3,256,256]{3,2,1,0:T(8,128)(2,1)} fusion(bf16[3,3,256,3072]{3,2,1,0:T(8,128)(2,1)S(1)} %bitcast.83, bf16[3072,256,1,1]{1,0,3,2:T(8,128)(2,1)S(1)} %bitcast.81), kind=kOutput, calls=%fused_computation.59 | convolution fusion | flops 3624468480 | bytes 16908288 | tf_op jit(solution)/shard_map/dot_general | solution.py:64
  155.2 3.0 %collective-permute-done.15 = bf16[1,50,256]{2,1,0:T(8,128)(2,1)S(1)} collective-permute-done((bf16[1,50,256]{2,1,0:T(8,128)(2,1)S(1)}, bf16[1,50,256]{2,1,0:T(8,128)(2,1)S(1)}, u32[]{:S(2)}, u32[]{:S(2)}) %collective-permute-start.15) | collective-permute-done | bytes 25632 | tf_op jit(solution)/shard_map/ppermute | solution.py:10
  158.3 3.7 %collective-permute-done.16 = bf16[1,50,256]{2,1,0:T(8,128)(2,1)S(1)} collective-permute-done((bf16[1,50,256]{2,1,0:T(8,128)(2,1)S(1)}, bf16[1,50,256]{2,1,0:T(8,128)(2,1)S(1)}, u32[]{:S(2)}, u32[]{:S(2)}) %collective-permute-start.16) | collective-permute-done | bytes 25632 | tf_op jit(solution)/shard_map/ppermute | solution.py:10
  162.0 5.9 %convolution_bitcast_fusion = f32[64,48,256]{2,1,0:T(8,128)} fusion(bf16[64,48,9,256]{3,1,0,2:T(8,128)(2,1)S(1)} %bitcast_dynamic-update-slice_fusion, bf16[9,256,256,1]{2,1,3,0:T(8,128)(2,1)S(1)} %bitcast.89), kind=kOutput, calls=%fused_computation.18 | convolution fusion | flops 3623878656 | bytes 18481152 | tf_op jit(solution)/shard_map/dot_general | solution.py:99
  168.2 1.9 fusion.27
  170.1 3.5 %fusion.10 = bf16[64,48,256]{2,1,0:T(8,128)(2,1)S(1)} fusion(f32[64,48,256]{2,1,0:T(8,128)} %fusion.27, bf16[64,48,256]{2,1,0:T(8,128)(2,1)S(1)} %copy-done.4, f32[64,48]{1,0:T(8,128)S(1)} %copy.9), kind=kLoop, calls=%fused_computation.15 | loop fusion | flops 9437184 | bytes 6303744 | tf_op jit(solution)/shard_map/convert_element_type | solution.py:108
  173.6 8.2 %convolution_convert_fusion.2 = bf16[3,3,256,256]{3,2,1,0:T(8,128)(2,1)} fusion(bf16[3,3,256,3072]{3,2,1,0:T(8,128)(2,1)} %bitcast.82, bf16[3072,256,1,1]{1,0,3,2:T(8,128)(2,1)S(1)} %bitcast.84), kind=kOutput, calls=%fused_computation.60 | convolution fusion | flops 3624468480 | bytes 16908288 | tf_op jit(solution)/shard_map/dot_general | solution.py:64
  181.8 99.3 %all-reduce.7.cloned.1.call-done = (bf16[3,3,256,256]{3,2,1,0:T(8,128)(2,1)}, bf16[3,3,256,256]{3,2,1,0:T(8,128)(2,1)}) async-done(((bf16[3,3,256,256]{3,2,1,0:T(8,128)(2,1)}, bf16[3,3,256,256]{3,2,1,0:T(8,128)(2,1)}), (bf16[3,3,256,256]{3,2,1,0:T(8,128)(2,1)}, bf16[3,3,256,256]{3,2,1,0:T(8,128)(2,1)})) %all-reduce.7.cloned.1.call-update) | async-done | bytes 2359312 | tf_op jit(solution)/shard_map/psum | solution.py:113
  281.1 3.0 %convert_element_type.46 = f32[3,3,256,256]{3,2,1,0:T(8,128)} convert(bf16[3,3,256,256]{3,2,1,0:T(8,128)(2,1)} %get-tuple-element.15) | non-fusion elementwise | flops 589824 | bytes 3538944 | tf_op jit(solution)/shard_map/convert_element_type | solution.py:113
  (87 shorter events, 31.6 us)
Async XLA Ops:
  7.2 36.7 %copy-start = (bf16[3,3,256,256]{3,2,1,0:T(8,128)(2,1)S(1)}, bf16[3,3,256,256]{3,2,1,0:T(8,128)(2,1)}, u32[]{:S(2)}) copy-start(bf16[3,3,256,256]{3,2,1,0:T(8,128)(2,1)} %param.10) | copy-start | bytes 3538948
  7.2 8.4 %copy-start.6 = (s32[64,48]{0,1:T(8,128)S(1)}, s32[64,48]{0,1:T(8,128)}, u32[]{:S(2)}) copy-start(s32[64,48]{0,1:T(8,128)} %param.9) | copy-start | bytes 36868
  7.2 273.9 %all-reduce.7.cloned.1.call-start = ((), (), s32[]{:S(2)}) async-start(), calls=%async_computation | async-start | bytes 4718592 | tf_op jit(solution)/shard_map/psum | solution.py:113
  10.0 7.6 %collective-permute-start = (bf16[64,1,256]{2,1,0:T(2,128)(2,1)S(1)}, bf16[64,1,256]{2,1,0:T(2,128)(2,1)S(1)}, u32[]{:S(2)}, u32[]{:S(2)}) collective-permute-start(bf16[64,1,256]{2,1,0:T(2,128)(2,1)S(1)} %get-tuple-element.23), channel_id=1, source_target_pairs={{0,1},{1,2},{2,3},{3,4},{4,5},{5,6},{6,7},{7,8},{8,9},{9,10},{10,1... | collective-permute-start | bytes 98312 | tf_op jit(solution)/shard_map/ppermute | solution.py:19
  10.5 7.1 %collective-permute-start.1 = (bf16[64,1,256]{2,1,0:T(2,128)(2,1)S(1)}, bf16[64,1,256]{2,1,0:T(2,128)(2,1)S(1)}, u32[]{:S(2)}, u32[]{:S(2)}) collective-permute-start(bf16[64,1,256]{2,1,0:T(2,128)(2,1)S(1)} %get-tuple-element.24), channel_id=1, source_target_pairs={{1,0},{2,1},{3,2},{4,3},{5,4},{6,5},{7,6},{8,7},{9,8},{10,9},{11,1... | collective-permute-start | bytes 98312 | tf_op jit(solution)/shard_map/ppermute | solution.py:22
  22.3 7.6 %copy-start.3 = (bf16[64,48,256]{2,1,0:T(8,128)(2,1)S(1)}, bf16[64,48,256]{2,1,0:T(8,128)(2,1)}, u32[]{:S(2)}) copy-start(bf16[64,48,256]{2,1,0:T(8,128)(2,1)} %param.7) | copy-start | bytes 4718596
  22.3 2.2 collective-permute-start.2
  24.5 3.9 %collective-permute-start.3 = (bf16[1,50,256]{2,1,0:T(8,128)(2,1)S(1)}, bf16[1,50,256]{2,1,0:T(8,128)(2,1)S(1)}, u32[]{:S(2)}, u32[]{:S(2)}) collective-permute-start(bf16[1,50,256]{2,1,0:T(8,128)(2,1)S(1)} %collective-permute-done.2), channel_id=1, source_target_pairs={{0,2},{1,3},{2,0},{3,1},{4,6},{5,7},{6,4},{7,5},{8,10},{9,11},{10,... | collective-permute-start | bytes 76808 | tf_op jit(solution)/shard_map/ppermute | solution.py:10
  28.4 3.9 %collective-permute-start.4 = (bf16[1,50,256]{2,1,0:T(8,128)(2,1)S(1)}, bf16[1,50,256]{2,1,0:T(8,128)(2,1)S(1)}, u32[]{:S(2)}, u32[]{:S(2)}) collective-permute-start(bf16[1,50,256]{2,1,0:T(8,128)(2,1)S(1)} %collective-permute-done.3), channel_id=1, source_target_pairs={{0,4},{1,5},{2,6},{3,7},{4,0},{5,1},{6,2},{7,3},{8,12},{9,13},{10,... | collective-permute-start | bytes 76808 | tf_op jit(solution)/shard_map/ppermute | solution.py:10
  32.2 4.8 %collective-permute-start.5 = (bf16[1,50,256]{2,1,0:T(8,128)(2,1)S(1)}, bf16[1,50,256]{2,1,0:T(8,128)(2,1)S(1)}, u32[]{:S(2)}, u32[]{:S(2)}) collective-permute-start(bf16[1,50,256]{2,1,0:T(8,128)(2,1)S(1)} %collective-permute-done.4), channel_id=1, source_target_pairs={{0,8},{1,9},{2,10},{3,11},{4,12},{5,13},{6,14},{7,15},{8,0},{9,1},... | collective-permute-start | bytes 76808 | tf_op jit(solution)/shard_map/ppermute | solution.py:10
  52.1 23.3 %collective-permute-start.6 = (bf16[64,1,256]{2,1,0:T(2,128)(2,1)S(1)}, bf16[64,1,256]{2,1,0:T(2,128)(2,1)S(1)}, u32[]{:S(2)}, u32[]{:S(2)}) collective-permute-start(bf16[64,1,256]{2,1,0:T(2,128)(2,1)S(1)} %get-tuple-element.21), channel_id=1, source_target_pairs={{0,1},{1,2},{2,3},{3,4},{4,5},{5,6},{6,7},{7,8},{8,9},{9,10},{10,1... | collective-permute-start | bytes 98312 | tf_op jit(solution)/shard_map/ppermute | solution.py:19
  52.1 23.3 %collective-permute-start.7 = (bf16[64,1,256]{2,1,0:T(2,128)(2,1)S(1)}, bf16[64,1,256]{2,1,0:T(2,128)(2,1)S(1)}, u32[]{:S(2)}, u32[]{:S(2)}) collective-permute-start(bf16[64,1,256]{2,1,0:T(2,128)(2,1)S(1)} %get-tuple-element.22), channel_id=1, source_target_pairs={{1,0},{2,1},{3,2},{4,3},{5,4},{6,5},{7,6},{8,7},{9,8},{10,9},{11,1... | collective-permute-start | bytes 98312 | tf_op jit(solution)/shard_map/ppermute | solution.py:22
  77.9 4.5 %collective-permute-start.8 = (bf16[1,50,256]{2,1,0:T(8,128)(2,1)S(1)}, bf16[1,50,256]{2,1,0:T(8,128)(2,1)S(1)}, u32[]{:S(2)}, u32[]{:S(2)}) collective-permute-start(bf16[1,50,256]{2,1,0:T(8,128)(2,1)S(1)} %slice.215), channel_id=1, source_target_pairs={{0,1},{1,0},{2,3},{3,2},{4,5},{5,4},{6,7},{7,6},{8,9},{9,8},{10,11... | collective-permute-start | bytes 76808 | tf_op jit(solution)/shard_map/ppermute | solution.py:10
  82.3 3.9 %collective-permute-start.9 = (bf16[1,50,256]{2,1,0:T(8,128)(2,1)S(1)}, bf16[1,50,256]{2,1,0:T(8,128)(2,1)S(1)}, u32[]{:S(2)}, u32[]{:S(2)}) collective-permute-start(bf16[1,50,256]{2,1,0:T(8,128)(2,1)S(1)} %collective-permute-done.8), channel_id=1, source_target_pairs={{0,2},{1,3},{2,0},{3,1},{4,6},{5,7},{6,4},{7,5},{8,10},{9,11},{10,... | collective-permute-start | bytes 76808 | tf_op jit(solution)/shard_map/ppermute | solution.py:10
  86.2 3.9 %collective-permute-start.10 = (bf16[1,50,256]{2,1,0:T(8,128)(2,1)S(1)}, bf16[1,50,256]{2,1,0:T(8,128)(2,1)S(1)}, u32[]{:S(2)}, u32[]{:S(2)}) collective-permute-start(bf16[1,50,256]{2,1,0:T(8,128)(2,1)S(1)} %collective-permute-done.9), channel_id=1, source_target_pairs={{0,4},{1,5},{2,6},{3,7},{4,0},{5,1},{6,2},{7,3},{8,12},{9,13},{10,... | collective-permute-start | bytes 76808 | tf_op jit(solution)/shard_map/ppermute | solution.py:10
  90.1 4.8 %collective-permute-start.11 = (bf16[1,50,256]{2,1,0:T(8,128)(2,1)S(1)}, bf16[1,50,256]{2,1,0:T(8,128)(2,1)S(1)}, u32[]{:S(2)}, u32[]{:S(2)}) collective-permute-start(bf16[1,50,256]{2,1,0:T(8,128)(2,1)S(1)} %collective-permute-done.10), channel_id=1, source_target_pairs={{0,8},{1,9},{2,10},{3,11},{4,12},{5,13},{6,14},{7,15},{8,0},{9,1},... | collective-permute-start | bytes 76808 | tf_op jit(solution)/shard_map/ppermute | solution.py:10
  101.7 18.8 %copy-start.7 = (bf16[64,48,256]{2,1,0:T(8,128)(2,1)S(1)}, bf16[64,48,256]{2,1,0:T(8,128)(2,1)}, u32[]{:S(2)}) copy-start(bf16[64,48,256]{2,1,0:T(8,128)(2,1)} %param.8) | copy-start | bytes 4718596
  101.7 18.8 %copy-start.8 = (bf16[3,3,256,256]{3,2,1,0:T(8,128)(2,1)S(1)}, bf16[3,3,256,256]{3,2,1,0:T(8,128)(2,1)}, u32[]{:S(2)}) copy-start(bf16[3,3,256,256]{3,2,1,0:T(8,128)(2,1)} %param.11) | copy-start | bytes 3538948
  120.5 23.4 %copy-start.2 = (bf16[2304,3072]{1,0:T(8,128)(2,1)S(1)}, bf16[2304,3072]{1,0:T(8,128)(2,1)}, u32[]{:S(2)}) copy-start(bf16[2304,3072]{1,0:T(8,128)(2,1)} %copy.12) | copy-start | bytes 42467332
  130.9 17.9 %collective-permute-start.12 = (bf16[64,1,256]{2,1,0:T(2,128)(2,1)S(1)}, bf16[64,1,256]{2,1,0:T(2,128)(2,1)S(1)}, u32[]{:S(2)}, u32[]{:S(2)}) collective-permute-start(bf16[64,1,256]{2,1,0:T(2,128)(2,1)S(1)} %get-tuple-element.19), channel_id=1, source_target_pairs={{0,1},{1,2},{2,3},{3,4},{4,5},{5,6},{6,7},{7,8},{8,9},{9,10},{10,1... | collective-permute-start | bytes 98312 | tf_op jit(solution)/shard_map/ppermute | solution.py:19
  131.0 17.8 %collective-permute-start.13 = (bf16[64,1,256]{2,1,0:T(2,128)(2,1)S(1)}, bf16[64,1,256]{2,1,0:T(2,128)(2,1)S(1)}, u32[]{:S(2)}, u32[]{:S(2)}) collective-permute-start(bf16[64,1,256]{2,1,0:T(2,128)(2,1)S(1)} %get-tuple-element.20), channel_id=1, source_target_pairs={{1,0},{2,1},{3,2},{4,3},{5,4},{6,5},{7,6},{8,7},{9,8},{10,9},{11,1... | collective-permute-start | bytes 98312 | tf_op jit(solution)/shard_map/ppermute | solution.py:22
  152.4 1.8 collective-permute-start.14
  154.2 7.8 %copy-start.9 = (bf16[3,3,256,256]{3,2,1,0:T(8,128)(2,1)S(1)}, bf16[3,3,256,256]{3,2,1,0:T(8,128)(2,1)}, u32[]{:S(2)}) copy-start(bf16[3,3,256,256]{3,2,1,0:T(8,128)(2,1)} %param.11) | copy-start | bytes 3538948
  154.2 3.9 %collective-permute-start.15 = (bf16[1,50,256]{2,1,0:T(8,128)(2,1)S(1)}, bf16[1,50,256]{2,1,0:T(8,128)(2,1)S(1)}, u32[]{:S(2)}, u32[]{:S(2)}) collective-permute-start(bf16[1,50,256]{2,1,0:T(8,128)(2,1)S(1)} %collective-permute-done.14), channel_id=1, source_target_pairs={{0,2},{1,3},{2,0},{3,1},{4,6},{5,7},{6,4},{7,5},{8,10},{9,11},{10,... | collective-permute-start | bytes 76808 | tf_op jit(solution)/shard_map/ppermute | solution.py:10
  158.2 3.9 %collective-permute-start.16 = (bf16[1,50,256]{2,1,0:T(8,128)(2,1)S(1)}, bf16[1,50,256]{2,1,0:T(8,128)(2,1)S(1)}, u32[]{:S(2)}, u32[]{:S(2)}) collective-permute-start(bf16[1,50,256]{2,1,0:T(8,128)(2,1)S(1)} %collective-permute-done.15), channel_id=1, source_target_pairs={{0,4},{1,5},{2,6},{3,7},{4,0},{5,1},{6,2},{7,3},{8,12},{9,13},{10,... | collective-permute-start | bytes 76808 | tf_op jit(solution)/shard_map/ppermute | solution.py:10
  162.0 5.9 %collective-permute-start.17 = (bf16[1,50,256]{2,1,0:T(8,128)(2,1)S(1)}, bf16[1,50,256]{2,1,0:T(8,128)(2,1)S(1)}, u32[]{:S(2)}, u32[]{:S(2)}) collective-permute-start(bf16[1,50,256]{2,1,0:T(8,128)(2,1)S(1)} %collective-permute-done.16), channel_id=1, source_target_pairs={{0,8},{1,9},{2,10},{3,11},{4,12},{5,13},{6,14},{7,15},{8,0},{9,1},... | collective-permute-start | bytes 76808 | tf_op jit(solution)/shard_map/ppermute | solution.py:10
  162.0 8.1 %copy-start.4 = (bf16[64,48,256]{2,1,0:T(8,128)(2,1)S(1)}, bf16[64,48,256]{2,1,0:T(8,128)(2,1)}, u32[]{:S(2)}) copy-start(bf16[64,48,256]{2,1,0:T(8,128)(2,1)} %get-tuple-element.29) | copy-start | bytes 4718596
  281.1 3.1 %copy-start.5 = (bf16[3,3,256,256]{3,2,1,0:T(8,128)(2,1)S(1)}, bf16[3,3,256,256]{3,2,1,0:T(8,128)(2,1)}, u32[]{:S(2)}) copy-start(bf16[3,3,256,256]{3,2,1,0:T(8,128)(2,1)} %get-tuple-element.16) | copy-start | bytes 3538948
  281.1 4.7 %copy-start.1 = (bf16[3,3,256,256]{3,2,1,0:T(8,128)(2,1)S(1)}, bf16[3,3,256,256]{3,2,1,0:T(8,128)(2,1)}, u32[]{:S(2)}) copy-start(bf16[3,3,256,256]{3,2,1,0:T(8,128)(2,1)} %param.10) | copy-start | bytes 3538948
Sparse Core Ops, SparseCore 0:
  181.9 99.0 all-reduce.6
where the time goes:
time: 298 us; the launch traced here: 293 us
  waiting for transfers between devices  115 us (39%)
  local copies, waits for them, and re-layouts  66 us (22%)
  matrix products  39.2 us (13%)
  starting transfers between devices  29.8 us (10%)
  other arithmetic  28.6 us (10%)
  between operations  14.5 us (5%)
    psum x1, waiting for transfers between devices, local(): lax.psum(terms_one.astype(jnp.bfloat16), 'lon').astype(jnp.float32)  99.3 us
    dot_general x2, local copies, waits for them, and re-layouts, kernel_terms(): lax.dot_general(patch_rows, error_rows, (((0,), (0,)), ((), ())), preferr...  37.4 us
    unnamed x37, local copies, waits for them, and re-layouts  23.3 us
    ppermute x3, starting transfers between devices, padded_2(): lax.ppermute(lax.slice_in_dim(block, 0, width, axis=dim), axis, backward)  22.6 us
    ppermute x12, waiting for transfers between devices, from_partner(): lax.ppermute(shard, axis, [(i, i ^ 1 << distance) for i in range(lax.axis...  13.6 us
    dot_general x2, matrix products, kernel_terms(): lax.dot_general(patch_rows, error_rows, (((0,), (0,)), ((), ())), preferr...  13.1 us
    unnamed x7, other arithmetic  12.1 us
    dot_general x1, matrix products, local(): jnp.dot(patches_two, kernel_two.reshape(9 * channels, channels), preferre...  10.3 us
  transfers between devices with their start and end apart: 19, of which 9 were waited for; matrix products, arithmetic and copies ran while one was open for 17% of the time, Pallas kernels for 0%

commit v1 on v0

v1 whole, which is shorter than its diff:
```python
import functools
import math

import jax
import jax.numpy as jnp
from jax import lax
from jax.experimental import pallas as pl
from jax.experimental.pallas import tpu as pltpu
from jax.sharding import PartitionSpec as P

F32, BF16 = jnp.float32, jnp.bfloat16
MESH = pl.DeviceIdType.MESH
ROWS = 8


def padded_rows(count, total):
    unit = 16 * count
    return -(-total // unit) * unit


def bit_orders(count):
    bits = list(range(count.bit_length() - 1))
    return bits, bits[:1] + bits[2:] + bits[1:2]


def kernel(
    n, height, width, ch,
    state, mask, k_one, target_hbm, k_two_hbm,
    pred_hbm, grad_one_hbm, grad_two_hbm,
    target, k_two, k_back, pred,
    x3, h3, e3, n3, xt, ht, slope, back,
    send_w, send_e, send_n, got_w, got_e, got_n, got_cw, got_ce,
    total, staged, landed, full,
    halo_send, halo_recv, sum_send, sum_recv, local_sem,
):
    me = lax.axis_index("lon")
    cells = height * width
    wide = 3 * ch
    step_rows = ROWS * width
    chunks = height // ROWS
    north_at = (height + 1) * width
    pad = total.shape[1]
    half = ch // 2
    orders = bit_orders(n)
    steps = len(orders[0])

    barrier = pltpu.get_barrier_semaphore()
    for k in range(1, n):
        pl.semaphore_signal(
            barrier, inc=1, device_id={"lon": lax.rem(me + k, n)}, device_id_type=MESH
        )
    load_target = pltpu.make_async_copy(target_hbm, target, local_sem.at[0])
    load_two = pltpu.make_async_copy(k_two_hbm, k_two, local_sem.at[1])
    load_two.start()
    load_target.start()

    flip = (
        lax.broadcasted_iota(jnp.int32, (width, width), 0)
        + lax.broadcasted_iota(jnp.int32, (width, width), 1)
        == width - 1
    ).astype(F32).astype(BF16)

    def mask_of(at, rows):
        m = mask[pl.ds(at, rows), :]
        return jnp.concatenate([m, m], axis=1)

    def send_halos(f):
        right, left = lax.rem(me + 1, n), lax.rem(me + n - 1, n)
        corner_w, corner_e = lax.rem(n - me, n), lax.rem(2 * n - 2 - me, n)

        def remote(src, dst, k, to):
            return pltpu.make_async_remote_copy(
                src_ref=src, dst_ref=dst, send_sem=halo_send.at[f, k], recv_sem=halo_recv.at[f, k],
                device_id={"lon": to}, device_id_type=MESH,
            )

        copies = [
            remote(send_e.at[f], got_w.at[f], 0, right),
            remote(send_w.at[f], got_e.at[f], 1, left),
            remote(send_n.at[f], got_n.at[f], 2, n - 1 - me),
        ]
        last = pl.ds(height - 8, 8)
        corners = [
            (remote(send_w.at[f, last], got_cw.at[f], 3, corner_w), corner_w, send_w, got_cw),
            (remote(send_e.at[f, last], got_ce.at[f], 4, corner_e), corner_e, send_e, got_ce),
        ]
        for copy in copies:
            copy.start()
        for copy, to, src, dst in corners:
            @pl.when(to != me)
            def _():
                copy.start()

            @pl.when(to == me)
            def _():
                dst[f] = src[f, last, :]

        def wait():
            for copy in copies:
                copy.wait()
            for copy, to, _, _ in corners:
                @pl.when(to != me)
                def _():
                    copy.wait()

        return wait

    def store_shifted(ref, at, values, rows):
        ref[pl.ds(at, rows), ch : 2 * ch] = values.astype(BF16)
        ref[pl.ds(at, rows), 0:ch] = pltpu.roll(values, 1, 0).astype(BF16)
        ref[pl.ds(at, rows), 2 * ch : wide] = pltpu.roll(values, rows - 1, 0).astype(BF16)

    tile_row = lax.broadcasted_iota(jnp.int32, (16, ch), 0)

    def patch(ref, f):
        def body(i, carry):
            first = pl.multiple_of((i + 1) * width, 16)
            last = pl.multiple_of((i + 2) * width - 16, 16)
            low = ref[pl.ds(first, 16), 0:ch].astype(F32)
            low = jnp.where(tile_row == 0, got_w[f, pl.ds(i, 1), :], low)
            ref[pl.ds(first, 16), 0:ch] = low.astype(BF16)
            high = ref[pl.ds(last, 16), 2 * ch : wide].astype(F32)
            high = jnp.where(tile_row == 15, got_e[f, pl.ds(i, 1), :], high)
            ref[pl.ds(last, 16), 2 * ch : wide] = high.astype(BF16)
            return carry

        lax.fori_loop(0, height, body, 0, unroll=8)

    row_at = lax.broadcasted_iota(jnp.int32, (width, ch), 0)

    def put_north(ref, at, f):
        row = got_n[f]
        ref[at : at + width, ch : 2 * ch] = row.astype(BF16)
        low = jnp.where(row_at == 0, got_cw[f, 7:8, :], pltpu.roll(row, 1, 0))
        high = jnp.where(row_at == width - 1, got_ce[f, 7:8, :], pltpu.roll(row, width - 1, 0))
        ref[at : at + width, 0:ch] = low.astype(BF16)
        ref[at : at + width, 2 * ch : wide] = high.astype(BF16)

    def edges(i, carry):
        first = pl.multiple_of(i * width, 16)
        last = pl.multiple_of((i + 1) * width - 16, 16)
        low = (state[pl.ds(first, 16), :] * mask_of(first, 16)).astype(F32)
        high = (state[pl.ds(last, 16), :] * mask_of(last, 16)).astype(F32)
        send_w[0, pl.ds(i, 1), :] = low[0:1, :]
        send_e[0, pl.ds(i, 1), :] = high[15:16, :]
        return carry

    lax.fori_loop(0, height, edges, 0, unroll=8)
    top = cells - width
    send_n[0] = jnp.dot(
        flip, state[top:cells, :] * mask_of(top, width), preferred_element_type=F32
    )
    pl.semaphore_wait(barrier, n - 1)
    wait_x = send_halos(0)

    for ref in (x3, h3, e3):
        ref[0:width, :] = jnp.zeros((width, wide), BF16)
    e3[north_at : north_at + width, :] = jnp.zeros((width, wide), BF16)
    back[0:width, :] = jnp.zeros((width, ch), BF16)
    back[north_at : north_at + width, :] = jnp.zeros((width, ch), BF16)
    if pad > 9 * ch:
        total[:, 9 * ch :, :] = jnp.zeros((2, pad - 9 * ch, ch), F32)

    def shift_state(c, carry):
        at = pl.multiple_of(c * step_rows, 16)
        values = (state[pl.ds(at, step_rows), :] * mask_of(at, step_rows)).astype(F32)
        store_shifted(x3, pl.multiple_of(at + width, 16), values, step_rows)
        return carry

    lax.fori_loop(0, chunks, shift_state, 0)

    load_two.wait()
    for a in range(3):
        for b in range(3):
            block = k_two[2 - a, (2 - b) * ch : (3 - b) * ch, :]
            k_back[a, b * ch : (b + 1) * ch, :] = block.T

    wait_x()
    patch(x3, 0)
    put_north(x3, north_at, 0)

    def conv(ref, weights, c):
        out = None
        for a in range(3):
            at = pl.multiple_of(c * step_rows + a * width, 16)
            term = jnp.dot(ref[pl.ds(at, step_rows), :], weights[a], preferred_element_type=F32)
            out = term if out is None else out + term
        return out

    def store_edges(f, c, values):
        for k in range(ROWS):
            i = c * ROWS + k
            send_w[f, pl.ds(i, 1), :] = values[k * width : k * width + 1, :]
            send_e[f, pl.ds(i, 1), :] = values[(k + 1) * width - 1 : (k + 1) * width, :]

    def layer_one(c, carry):
        at = pl.multiple_of(c * step_rows, 16)
        u = conv(x3, k_one, c).astype(BF16).astype(F32)
        m = mask_of(at, step_rows).astype(F32)
        cdf = 0.5 + 0.5 * lax.erf(u * (1.0 / math.sqrt(2.0)))
        density = jnp.exp(-0.5 * u * u) * (1.0 / math.sqrt(2.0 * math.pi))
        hidden = (u * cdf * m).astype(BF16).astype(F32)
        slope[pl.ds(at, step_rows), :] = (cdf + u * density) * m
        store_shifted(h3, pl.multiple_of(at + width, 16), hidden, step_rows)
        store_edges(1, c, hidden)
        return carry

    lax.fori_loop(0, chunks, layer_one, 0)
    send_n[1] = jnp.dot(flip, h3[cells : cells + width, ch : 2 * ch], preferred_element_type=F32)
    wait_h = send_halos(1)

    def transpose(ref, out):
        def body(c, carry):
            at = pl.multiple_of(c * step_rows, 128)
            for b in range(3):
                piece = ref[pl.ds(pl.multiple_of(at + width, 16), step_rows), b * ch : (b + 1) * ch]
                out[b * ch : (b + 1) * ch, pl.ds(at, step_rows)] = piece.T
            return carry

        lax.fori_loop(0, chunks, body, 0)
        out[:, cells : cells + width] = ref[north_at : north_at + width, :].T

    transpose(x3, xt)
    wait_h()
    patch(h3, 1)
    put_north(h3, north_at, 1)
    load_target.wait()
    scale = 1.0 / math.sqrt(cells * n)

    def layer_two(c, carry):
        at = pl.multiple_of(c * step_rows, 16)
        out = conv(h3, k_two, c)
        m = mask_of(at, step_rows).astype(F32)
        pred[pl.ds(at, step_rows), :] = (out * m).astype(BF16)
        error = m * (out - target[pl.ds(at, step_rows), :].astype(F32)) * scale
        error = error.astype(BF16).astype(F32)
        store_shifted(e3, pl.multiple_of(at + width, 16), error, step_rows)
        store_edges(2, c, error)
        return carry

    lax.fori_loop(0, chunks, layer_two, 0)
    send_n[2] = jnp.dot(flip, e3[cells : cells + width, ch : 2 * ch], preferred_element_type=F32)
    wait_e = send_halos(2)
    store_pred = pltpu.make_async_copy(pred, pred_hbm, local_sem.at[2])
    store_pred.start()

    def kernel_grad(g, a, field_t, error, lanes):
        depth = cells + (width if a == 2 else 0)
        at = (2 - a) * width
        total[g, a * wide : (a + 1) * wide, :] = jnp.dot(
            field_t[:, 0:depth], error[at : at + depth, lanes], preferred_element_type=F32
        )

    starts = [[0, 0], [0, 0]]
    flying = {}

    def partner(h, s):
        bit = 1 << orders[h][s]
        mine = lax.rem(me // bit, 2)
        return mine, me + (1 - 2 * mine) * bit

    def send_half(g, s):
        size = pad >> (s + 1)
        offset = pad - (pad >> s)
        for h in range(2):
            mine, to = partner(h, s)
            lanes = slice(h * half, (h + 1) * half)
            away = pl.multiple_of(starts[g][h] + (1 - mine) * size, 16)
            staged[g, h, offset : offset + size, :] = total[g, pl.ds(away, size), lanes].astype(BF16)
            copy = pltpu.make_async_remote_copy(
                src_ref=staged.at[g, h, pl.ds(offset, size)],
                dst_ref=landed.at[g, h, pl.ds(offset, size)],
                send_sem=sum_send.at[g, s, h], recv_sem=sum_recv.at[g, s, h],
                device_id={"lon": to}, device_id_type=MESH,
            )
            copy.start()
            flying[g, h] = copy
            starts[g][h] = starts[g][h] + mine * size

    def add_half(g, s):
        size = pad >> (s + 1)
        offset = pad - (pad >> s)
        for h in range(2):
            lanes = slice(h * half, (h + 1) * half)
            flying[g, h].wait()
            at = pl.ds(pl.multiple_of(starts[g][h], 16), size)
            total[g, at, lanes] = total[g, at, lanes] + landed[
                g, h, offset : offset + size, :
            ].astype(F32)

    def round_own(g):
        size = pad >> steps
        for h in range(2):
            lanes = slice(h * half, (h + 1) * half)
            at = pl.ds(pl.multiple_of(starts[g][h], 16), size)
            full[g, at, lanes] = total[g, at, lanes].astype(BF16)

    def send_own(g, s):
        size = pad >> (s + 1)
        for h in range(2):
            mine, to = partner(h, s)
            at = pl.ds(pl.multiple_of(starts[g][h], 16), size)
            own = full.at[g, at, pl.ds(h * half, half)]
            copy = pltpu.make_async_remote_copy(
                src_ref=own, dst_ref=own,
                send_sem=sum_send.at[g, 2 * steps - 1 - s, h],
                recv_sem=sum_recv.at[g, 2 * steps - 1 - s, h],
                device_id={"lon": to}, device_id_type=MESH,
            )
            copy.start()
            flying[g, h] = copy
            starts[g][h] = starts[g][h] - mine * size

    def wait_own(g):
        for h in range(2):
            flying[g, h].wait()

    def sum_stages(g):
        for s in range(steps):
            send_half(g, s)
            yield
            add_half(g, s)
        round_own(g)
        for s in reversed(range(steps)):
            send_own(g, s)
            yield
            wait_own(g)

    transpose(h3, ht)
    middle = slice(ch, 2 * ch)
    for a in range(3):
        kernel_grad(1, a, ht, e3, middle)
    sum_two = sum_stages(1)
    next(sum_two)

    wait_e()
    patch(e3, 2)
    put_north(n3, 0, 2)
    fold = None
    for b in range(3):
        term = jnp.dot(
            n3[:, b * ch : (b + 1) * ch], k_back[0, (2 - b) * ch : (3 - b) * ch, :],
            preferred_element_type=F32,
        )
        fold = term if fold is None else fold + term

    def pull_back(c, carry, extra=None):
        at = pl.multiple_of(c * step_rows, 16)
        grad = conv(e3, k_back, c)
        if extra is not None:
            grad = grad + extra
        grad = grad * slope[pl.ds(at, step_rows), :]
        back[pl.ds(pl.multiple_of(at + width, 16), step_rows), :] = grad.astype(BF16)
        return carry

    last = jnp.concatenate([jnp.zeros((step_rows - width, ch), F32), fold], axis=0)
    pull_back(chunks - 1, 0, last)
    groups = 3
    edges_at = [(chunks - 1) * k // groups for k in range(groups + 1)]
    for k in range(groups):
        lax.fori_loop(edges_at[k], edges_at[k + 1], pull_back, 0)
        next(sum_two)
    for a in range(3):
        kernel_grad(0, a, xt, back, slice(None))
        next(sum_two)
    sum_one = sum_stages(0)
    for _ in sum_one:
        next(sum_two, None)
    for _ in sum_two:
        pass
    stores = [
        pltpu.make_async_copy(full.at[0], grad_one_hbm, local_sem.at[3]),
        pltpu.make_async_copy(full.at[1], grad_two_hbm, local_sem.at[4]),
    ]
    for store in stores:
        store.start()
    store_pred.wait()
    for store in stores:
        store.wait()


def local(n, state_in, target, ocean_mask, kernel_one, kernel_two):
    height, width, ch = state_in.shape
    cells, wide = height * width, 3 * ch
    ext = (height + 2) * width
    pad = padded_rows(n, 9 * ch)
    steps = n.bit_length() - 1
    deep = -(-(cells + width) // 128) * 128
    mask = jnp.broadcast_to(
        ocean_mask.astype(BF16)[..., None], (height, width, ch // 2)
    ).reshape(cells, ch // 2)
    vmem, anywhere = pl.BlockSpec(memory_space=pltpu.VMEM), pl.BlockSpec(memory_space=pl.ANY)
    dma = pltpu.SemaphoreType.DMA
    prediction, grad_one, grad_two = pl.pallas_call(
        functools.partial(kernel, n, height, width, ch),
        out_shape=(
            jax.ShapeDtypeStruct((cells, ch), BF16),
            jax.ShapeDtypeStruct((pad, ch), BF16),
            jax.ShapeDtypeStruct((pad, ch), BF16),
        ),
        in_specs=[vmem, vmem, vmem, anywhere, anywhere],
        out_specs=(anywhere, anywhere, anywhere),
        scratch_shapes=[
            pltpu.VMEM((cells, ch), BF16),
            pltpu.VMEM((3, wide, ch), BF16),
            pltpu.VMEM((3, wide, ch), BF16),
            pltpu.VMEM((cells, ch), BF16),
            pltpu.VMEM((ext, wide), BF16),
            pltpu.VMEM((ext, wide), BF16),
            pltpu.VMEM((ext, wide), BF16),
            pltpu.VMEM((width, wide), BF16),
            pltpu.VMEM((wide, deep), BF16),
            pltpu.VMEM((wide, deep), BF16),
            pltpu.VMEM((cells, ch), F32),
            pltpu.VMEM((ext, ch), BF16),
            pltpu.VMEM((3, height, ch), F32),
            pltpu.VMEM((3, height, ch), F32),
            pltpu.VMEM((3, width, ch), F32),
            pltpu.VMEM((3, height, ch), F32),
            pltpu.VMEM((3, height, ch), F32),
            pltpu.VMEM((3, width, ch), F32),
            pltpu.VMEM((3, 8, ch), F32),
            pltpu.VMEM((3, 8, ch), F32),
            pltpu.VMEM((2, pad, ch), F32),
            pltpu.VMEM((2, 2, pad, ch // 2), BF16),
            pltpu.VMEM((2, 2, pad, ch // 2), BF16),
            pltpu.VMEM((2, pad, ch), BF16),
            dma((3, 5)),
            dma((3, 5)),
            dma((2, 2 * steps, 2)),
            dma((2, 2 * steps, 2)),
            dma((5,)),
        ],
        compiler_params=pltpu.CompilerParams(
            collective_id=0, has_side_effects=True, vmem_limit_bytes=60 * 1024 * 1024
        ),
        cost_estimate=pl.CostEstimate(
            flops=10 * cells * 9 * ch * ch, bytes_accessed=16 * cells * ch, transcendentals=2 * cells * ch
        ),
    )(
        state_in.reshape(cells, ch),
        mask,
        kernel_one.reshape(3, wide, ch),
        target.reshape(cells, ch),
        kernel_two.reshape(3, wide, ch),
    )
    shape = (3, 3, ch, ch)
    return (
        prediction.reshape(height, width, ch),
        grad_one[: 9 * ch].astype(F32).reshape(shape),
        grad_two[: 9 * ch].astype(F32).reshape(shape),
    )


def solution(mesh):
    return jax.shard_map(
        functools.partial(local, mesh.shape["lon"]),
        mesh=mesh,
        in_specs=(P("groups", "lon", None), P("groups", "lon", None), P("groups", "lon"), P(), P()),
        out_specs=(
            P("groups", "lon", None),
            P("groups", None, None, None),
            P("groups", None, None, None),
        ),
        check_vma=False,
    )
```

time: 298 us -> 107 us (0.36); the launches traced: 293 us -> 107 us
  waiting for transfers between devices: 115 us -> 0 us
  Pallas kernels: 0 us -> 98 us
  local copies, waits for them, and re-layouts: 66 us -> 3.08 us
  matrix products: 39.2 us -> 0 us
  starting transfers between devices: 29.8 us -> 0 us
  other arithmetic: 28.6 us -> 5.36 us
  between operations: 14.5 us -> 0.65 us
    psum x1 -> x0, waiting for transfers between devices: 99.3 us -> none  [local(): lax.psum(terms_one.astype(jnp.bfloat16), 'lon').astype(jnp.float32)]
    pallas_call x0 -> x1, Pallas kernels: none -> 98 us  [local(): pl.pallas_call(functools.partial(kernel, n, height, width, ch), out_shape...]
    dot_general x6 -> x0, matrix products: 39.2 us -> none  [the longest x2 13.1 us: kernel_terms(): lax.dot_general(patch_rows, error_rows, (((0,), (0,)), ((), ())), preferr...]
    dot_general x2 -> x0, local copies, waits for them, and re-layouts: 37.4 us -> none  [kernel_terms(): lax.dot_general(patch_rows, error_rows, (((0,), (0,)), ((), ())), preferr...]
    ppermute x18 -> x0, starting transfers between devices: 29.8 us -> none  [the longest x3 22.6 us: padded_2(): lax.ppermute(lax.slice_in_dim(block, 0, width, axis=dim), axis, backward)]
    unnamed x37 -> x5, local copies, waits for them, and re-layouts: 23.3 us -> 1.52 us
    ppermute x18 -> x0, waiting for transfers between devices: 15.5 us -> none  [the longest x12 13.6 us: from_partner(): lax.ppermute(shard, axis, [(i, i ^ 1 << distance) for i in range(lax.axis...]
    unnamed x7 -> x0, other arithmetic: 12.1 us -> none
  transfers between devices with their start and end apart: 19 -> 0, of which waited for: 9 -> 0; matrix products, arithmetic and copies ran while one was open for 17% -> 0% of each run, Pallas kernels for 0% -> 0%
where the time goes in v1:
time: 107 us
  Pallas kernels  98 us (92%)
  other arithmetic  5.36 us (5%)
  local copies, waits for them, and re-layouts  3.08 us (3%)
    pallas_call x1, Pallas kernels, local(): pl.pallas_call(functools.partial(kernel, n, height, width, ch), out_shape...  98 us
    reshape x1, other arithmetic, local(): grad_one[:9 * ch].astype(F32).reshape(shape)  2.99 us

profile of v1, /device:TPU:0, one launch (start us, length us, event | category | flops | bytes accessed | tf_op | source)
XLA Modules:
  0.0 107.1 jit_solution(449588406895240393)
XLA Ops:
  0.6 0.7 convert_element_type.2
  1.4 0.1 copy.8
  1.5 0.1 broadcast_in_dim.8
  1.6 1.4 %broadcast_in_dim.9.mask = bf16[3072,128]{1,0:T(8,128)(2,1)} broadcast(bf16[3072]{0:T(1024)(128)(2,1)S(1)} %broadcast_in_dim.8), dimensions={0} | broadcast | bytes 792576 | tf_op jit(solution)/shard_map/broadcast_in_dim | solution.py:389
  2.9 98.0 %shard_map.76 = (bf16[3072,256]{1,0:T(8,128)(2,1)}, bf16[2304,256]{1,0:T(8,128)(2,1)}, bf16[2304,256]{1,0:T(8,128)(2,1)}) custom-call(bf16[3072,256]{1,0:T(8,128)(2,1)} %bitcast.12, bf16[3072,128]{1,0:T(8,128)(2,1)} %broadcast_in_dim.9.mask, bf16[3,768,256]{2,1,0:T(8,128)(2,1)} %bitcast.14, bf16[3072,256]{1,0:T(8,128)(2,1)} %bitcast.13, ...), custom_call_target="tpu_custom_call" | custom-call | flops 18119393280 | bytes 12582912 | tf_op jit(solution)/shard_map/pallas_call | solution.py:394
  101.0 0.0 copy-start.1
  101.0 3.0 %convert.2 = f32[3,3,256,256]{3,2,1,0:T(8,128)} convert(bf16[3,3,256,256]{3,2,1,0:T(8,128)(2,1)} %bitcast.11) | non-fusion elementwise | flops 589824 | bytes 3538944 | tf_op jit(solution)/shard_map/reshape | solution.py:450
  104.0 0.0 copy-done.1
  104.0 0.0 copy-start
  104.0 1.6 %convert.3 = f32[3,3,256,256]{3,2,1,0:T(8,128)} convert(bf16[3,3,256,256]{3,2,1,0:T(8,128)(2,1)S(1)} %bitcast.10) | non-fusion elementwise | flops 589824 | bytes 3538944 | tf_op jit(solution)/shard_map/reshape | solution.py:451
  105.6 0.4 copy-done
  106.0 1.1 %copy.10 = bf16[64,48,256]{2,1,0:T(8,128)(2,1)} copy(bf16[64,48,256]{2,1,0:T(8,128)(2,1)S(1)} %bitcast.9) | data formatting | bytes 3145728
Async XLA Ops:
  101.0 3.0 %copy-start.1 = (bf16[2304,256]{1,0:T(8,128)(2,1)S(1)}, bf16[2304,256]{1,0:T(8,128)(2,1)}, u32[]{:S(2)}) copy-start(bf16[2304,256]{1,0:T(8,128)(2,1)} %get-tuple-element.8) | copy-start | bytes 3538948
  104.0 2.0 %copy-start = (bf16[3072,256]{1,0:T(8,128)(2,1)S(1)}, bf16[3072,256]{1,0:T(8,128)(2,1)}, u32[]{:S(2)}) copy-start(bf16[3072,256]{1,0:T(8,128)(2,1)} %get-tuple-element.6) | copy-start | bytes 4718596

commit v2 on v1

v2 whole, which is shorter than its diff:
```python
import functools
import math

import jax
import jax.numpy as jnp
from jax import lax
from jax.experimental import pallas as pl
from jax.experimental.pallas import tpu as pltpu
from jax.sharding import PartitionSpec as P

F32, BF16 = jnp.float32, jnp.bfloat16
MESH = pl.DeviceIdType.MESH
ROWS = 8


def padded_rows(count, total):
    unit = 16 * count
    return -(-total // unit) * unit


def bit_orders(count):
    bits = list(range(count.bit_length() - 1))
    return bits, bits[:1] + bits[2:] + bits[1:2]


def kernel(
    n, height, width, ch,
    state, ocean, k_one_hbm, target_hbm, k_two_hbm,
    pred_hbm, grad_one_hbm, grad_two_hbm,
    mask, target, k_one, k_two, k_back, pred,
    x3, h3, e3, n3, xt, ht, slope, back,
    send_w, send_e, send_n, got_w, got_e, got_n, got_cw, got_ce,
    total, staged, landed, full,
    halo_send, halo_recv, sum_send, sum_recv, local_sem,
):
    me = lax.axis_index("lon")
    cells = height * width
    wide = 3 * ch
    step_rows = ROWS * width
    chunks = height // ROWS
    north_at = (height + 1) * width
    pad = total.shape[2]
    half = ch // 2
    orders = bit_orders(n)
    steps = len(orders[0])

    barrier = pltpu.get_barrier_semaphore()
    for k in range(1, n):
        pl.semaphore_signal(
            barrier, inc=1, device_id={"lon": lax.rem(me + k, n)}, device_id_type=MESH
        )
    load_target = pltpu.make_async_copy(target_hbm, target, local_sem.at[0])
    load_two = pltpu.make_async_copy(k_two_hbm, k_two, local_sem.at[1])
    load_one = pltpu.make_async_copy(k_one_hbm, k_one, local_sem.at[5])
    load_one.start()
    load_two.start()
    load_target.start()

    flip = (
        lax.broadcasted_iota(jnp.int32, (width, width), 0)
        + lax.broadcasted_iota(jnp.int32, (width, width), 1)
        == width - 1
    ).astype(F32).astype(BF16)

    def mask_of(at, rows):
        m = mask[pl.ds(at, rows), :]
        return jnp.concatenate([m, m], axis=1)

    eye = (
        lax.broadcasted_iota(jnp.int32, (width, width), 0)
        == lax.broadcasted_iota(jnp.int32, (width, width), 1)
    ).astype(F32)
    eyes = jnp.concatenate([eye] * ROWS, axis=0)
    cell_at = lax.broadcasted_iota(jnp.int32, (step_rows, ROWS), 0)
    row_of = lax.broadcasted_iota(jnp.int32, (step_rows, ROWS), 1) * width
    pick = ((cell_at >= row_of) & (cell_at < row_of + width)).astype(F32)
    for c in range(chunks):
        part = ocean[c * ROWS : (c + 1) * ROWS, :].astype(F32)
        part = jnp.dot(pick, part, preferred_element_type=F32) * eyes
        part = jnp.dot(part, jnp.ones((width, half), F32), preferred_element_type=F32)
        mask[c * step_rows : (c + 1) * step_rows, :] = part.astype(BF16)

    def send_halos(f, q, lo, hi):
        north = hi == height
        right, left = lax.rem(me + 1, n), lax.rem(me + n - 1, n)
        corner_w, corner_e = lax.rem(n - me, n), lax.rem(2 * n - 2 - me, n)

        def remote(src, dst, k, to):
            return pltpu.make_async_remote_copy(
                src_ref=src, dst_ref=dst, send_sem=halo_send.at[q, k], recv_sem=halo_recv.at[q, k],
                device_id={"lon": to}, device_id_type=MESH,
            )

        span = pl.ds(lo, hi - lo)
        copies = [
            remote(send_e.at[f, span], got_w.at[f, span], 0, right),
            remote(send_w.at[f, span], got_e.at[f, span], 1, left),
        ]
        if north:
            copies.append(remote(send_n.at[f], got_n.at[f], 2, n - 1 - me))
        last = pl.ds(height - 8, 8)
        corners = [
            (remote(send_w.at[f, last], got_cw.at[f], 3, corner_w), corner_w, send_w, got_cw),
            (remote(send_e.at[f, last], got_ce.at[f], 4, corner_e), corner_e, send_e, got_ce),
        ] if north else []
        for copy in copies:
            copy.start()
        for copy, to, src, dst in corners:
            @pl.when(to != me)
            def _():
                copy.start()

            @pl.when(to == me)
            def _():
                dst[f] = src[f, last, :]

        def wait():
            for copy in copies:
                copy.wait()
            for copy, to, _, _ in corners:
                @pl.when(to != me)
                def _():
                    copy.wait()

        return wait

    def store_shifted(ref, at, values, rows):
        ref[pl.ds(at, rows), ch : 2 * ch] = values.astype(BF16)
        ref[pl.ds(at, rows), 0:ch] = pltpu.roll(values, 1, 0).astype(BF16)
        ref[pl.ds(at, rows), 2 * ch : wide] = pltpu.roll(values, rows - 1, 0).astype(BF16)

    tile_row = lax.broadcasted_iota(jnp.int32, (16, ch), 0)

    def patch(ref, f, lo, hi):
        def body(i, carry):
            first = pl.multiple_of((i + 1) * width, 16)
            last = pl.multiple_of((i + 2) * width - 16, 16)
            low = ref[pl.ds(first, 16), 0:ch].astype(F32)
            low = jnp.where(tile_row == 0, got_w[f, pl.ds(i, 1), :], low)
            ref[pl.ds(first, 16), 0:ch] = low.astype(BF16)
            high = ref[pl.ds(last, 16), 2 * ch : wide].astype(F32)
            high = jnp.where(tile_row == 15, got_e[f, pl.ds(i, 1), :], high)
            ref[pl.ds(last, 16), 2 * ch : wide] = high.astype(BF16)
            return carry

        lax.fori_loop(lo, hi, body, 0, unroll=8)

    row_at = lax.broadcasted_iota(jnp.int32, (width, ch), 0)

    def put_north(ref, at, f):
        row = got_n[f]
        ref[at : at + width, ch : 2 * ch] = row.astype(BF16)
        low = jnp.where(row_at == 0, got_cw[f, 7:8, :], pltpu.roll(row, 1, 0))
        high = jnp.where(row_at == width - 1, got_ce[f, 7:8, :], pltpu.roll(row, width - 1, 0))
        ref[at : at + width, 0:ch] = low.astype(BF16)
        ref[at : at + width, 2 * ch : wide] = high.astype(BF16)

    def edges(i, carry):
        first = pl.multiple_of(i * width, 16)
        last = pl.multiple_of((i + 1) * width - 16, 16)
        low = (state[pl.ds(first, 16), :] * mask_of(first, 16)).astype(F32)
        high = (state[pl.ds(last, 16), :] * mask_of(last, 16)).astype(F32)
        send_w[0, pl.ds(i, 1), :] = low[0:1, :]
        send_e[0, pl.ds(i, 1), :] = high[15:16, :]
        return carry

    lax.fori_loop(0, height, edges, 0, unroll=8)
    top = cells - width
    send_n[0] = jnp.dot(
        flip, state[top:cells, :] * mask_of(top, width), preferred_element_type=F32
    )
    pl.semaphore_wait(barrier, n - 1)
    wait_x = send_halos(0, 0, 0, height)

    for ref in (x3, h3, e3):
        ref[0:width, :] = jnp.zeros((width, wide), BF16)
    e3[north_at : north_at + width, :] = jnp.zeros((width, wide), BF16)
    back[0:width, :] = jnp.zeros((width, ch), BF16)
    back[north_at : north_at + width, :] = jnp.zeros((width, ch), BF16)
    if pad > wide:
        total[:, :, wide:, :] = jnp.zeros((2, 3, pad - wide, ch), F32)

    def shift_state(c, carry):
        at = pl.multiple_of(c * step_rows, 16)
        values = (state[pl.ds(at, step_rows), :] * mask_of(at, step_rows)).astype(F32)
        store_shifted(x3, pl.multiple_of(at + width, 16), values, step_rows)
        return carry

    lax.fori_loop(0, chunks, shift_state, 0)

    load_two.wait()
    for a in range(3):
        for b in range(3):
            block = k_two[2 - a, (2 - b) * ch : (3 - b) * ch, :]
            k_back[a, b * ch : (b + 1) * ch, :] = block.T

    wait_x()
    patch(x3, 0, 0, height)
    put_north(x3, north_at, 0)
    load_one.wait()

    def conv(ref, weights, c):
        out = None
        for a in range(3):
            at = c * step_rows + a * width
            term = jnp.dot(ref[at : at + step_rows, :], weights[a], preferred_element_type=F32)
            out = term if out is None else out + term
        return out

    def store_edges(f, c, values):
        for k in range(ROWS):
            i = c * ROWS + k
            send_w[f, i : i + 1, :] = values[k * width : k * width + 1, :]
            send_e[f, i : i + 1, :] = values[(k + 1) * width - 1 : (k + 1) * width, :]

    def transpose(ref, out, c):
        at = c * step_rows
        for b in range(3):
            piece = ref[at + width : at + width + step_rows, b * ch : (b + 1) * ch]
            out[b * ch : (b + 1) * ch, at : at + step_rows] = piece.T

    def transpose_north(ref, out):
        out[:, cells : cells + width] = ref[north_at : north_at + width, :].T

    def layer_one(c):
        at = c * step_rows
        u = conv(x3, k_one, c).astype(BF16).astype(F32)
        transpose(x3, xt, c)
        m = mask_of(at, step_rows).astype(F32)
        cdf = 0.5 + 0.5 * lax.erf(u * (1.0 / math.sqrt(2.0)))
        density = jnp.exp(-0.5 * u * u) * (1.0 / math.sqrt(2.0 * math.pi))
        hidden = (u * cdf * m).astype(BF16).astype(F32)
        slope[at : at + step_rows, :] = (cdf + u * density) * m
        store_shifted(h3, at + width, hidden, step_rows)
        store_edges(1, c, hidden)

    split = chunks // 2
    for c in range(split):
        layer_one(c)
    wait_low = send_halos(1, 1, 0, split * ROWS)
    for c in range(split, chunks):
        layer_one(c)
    send_n[1] = jnp.dot(flip, h3[cells : cells + width, ch : 2 * ch], preferred_element_type=F32)
    wait_high = send_halos(1, 3, split * ROWS, height)
    transpose_north(x3, xt)
    scale = 1.0 / math.sqrt(cells * n)

    def layer_two(c):
        at = c * step_rows
        out = conv(h3, k_two, c)
        transpose(h3, ht, c)
        m = mask_of(at, step_rows).astype(F32)
        pred[at : at + step_rows, :] = (out * m).astype(BF16)
        error = m * (out - target[at : at + step_rows, :].astype(F32)) * scale
        error = error.astype(BF16).astype(F32)
        store_shifted(e3, at + width, error, step_rows)
        store_edges(2, c, error)

    load_target.wait()
    wait_low()
    patch(h3, 1, 0, split * ROWS)
    for c in range(split - 1):
        layer_two(c)
    wait_high()
    patch(h3, 1, split * ROWS, height)
    put_north(h3, north_at, 1)
    for c in range(split - 1, chunks):
        layer_two(c)
    send_n[2] = jnp.dot(flip, e3[cells : cells + width, ch : 2 * ch], preferred_element_type=F32)
    wait_e = send_halos(2, 2, 0, height)
    transpose_north(h3, ht)
    store_pred = pltpu.make_async_copy(pred, pred_hbm, local_sem.at[2])
    store_pred.start()

    def kernel_grad(g, a, field_t, error, lanes):
        depth = cells + (width if a == 2 else 0)
        at = (2 - a) * width
        total[g, a, 0:wide, :] = jnp.dot(
            field_t[:, 0:depth], error[at : at + depth, lanes], preferred_element_type=F32
        )

    def partner(h, s):
        bit = 1 << orders[h][s]
        mine = lax.rem(me // bit, 2)
        return mine, me + (1 - 2 * mine) * bit

    def sum_stages(g, p):
        starts = [0, 0]
        lanes = [slice(h * half, (h + 1) * half) for h in range(2)]
        for s in range(steps):
            size = pad >> (s + 1)
            offset = pad - (pad >> s)
            flying = []
            for h in range(2):
                mine, to = partner(h, s)
                away = pl.multiple_of(starts[h] + (1 - mine) * size, 16)
                staged[g, p, h, offset : offset + size, :] = total[
                    g, p, pl.ds(away, size), lanes[h]
                ].astype(BF16)
                copy = pltpu.make_async_remote_copy(
                    src_ref=staged.at[g, p, h, pl.ds(offset, size)],
                    dst_ref=landed.at[g, p, h, pl.ds(offset, size)],
                    send_sem=sum_send.at[g, p, s, h], recv_sem=sum_recv.at[g, p, s, h],
                    device_id={"lon": to}, device_id_type=MESH,
                )
                copy.start()
                flying.append(copy)
                starts[h] = starts[h] + mine * size
            yield
            for h in range(2):
                flying[h].wait()
                at = pl.ds(pl.multiple_of(starts[h], 16), size)
                total[g, p, at, lanes[h]] = total[g, p, at, lanes[h]] + landed[
                    g, p, h, offset : offset + size, :
                ].astype(F32)
        for h in range(2):
            at = pl.ds(pl.multiple_of(starts[h], 16), pad >> steps)
            full[g, p, at, lanes[h]] = total[g, p, at, lanes[h]].astype(BF16)
        for s in reversed(range(steps)):
            size = pad >> (s + 1)
            slot = 2 * steps - 1 - s
            flying = []
            for h in range(2):
                mine, to = partner(h, s)
                at = pl.ds(pl.multiple_of(starts[h], 16), size)
                own = full.at[g, p, at, pl.ds(h * half, half)]
                copy = pltpu.make_async_remote_copy(
                    src_ref=own, dst_ref=own,
                    send_sem=sum_send.at[g, p, slot, h], recv_sem=sum_recv.at[g, p, slot, h],
                    device_id={"lon": to}, device_id_type=MESH,
                )
                copy.start()
                flying.append(copy)
                starts[h] = starts[h] - mine * size
            yield
            for copy in flying:
                copy.wait()

    sums = []

    def advance():
        sums[:] = [one for one in sums if next(one, True) is None]

    middle = slice(ch, 2 * ch)
    for a in range(3):
        kernel_grad(1, a, ht, e3, middle)
        sums.append(sum_stages(1, a))
        advance()

    wait_e()
    patch(e3, 2, 0, height)
    put_north(n3, 0, 2)
    fold = None
    for b in range(3):
        term = jnp.dot(
            n3[:, b * ch : (b + 1) * ch], k_back[0, (2 - b) * ch : (3 - b) * ch, :],
            preferred_element_type=F32,
        )
        fold = term if fold is None else fold + term
    fold = jnp.concatenate([jnp.zeros((step_rows - width, ch), F32), fold], axis=0)

    for c in range(chunks):
        at = c * step_rows
        grad = conv(e3, k_back, c)
        if c == chunks - 1:
            grad = grad + fold
        grad = grad * slope[at : at + step_rows, :]
        back[at + width : at + width + step_rows, :] = grad.astype(BF16)
        if c in (chunks // 2 - 1, chunks - 1):
            advance()
    for a in range(3):
        kernel_grad(0, a, xt, back, slice(None))
        sums.append(sum_stages(0, a))
        advance()
    while sums:
        advance()
    stores = [
        pltpu.make_async_copy(full.at[0], grad_one_hbm, local_sem.at[3]),
        pltpu.make_async_copy(full.at[1], grad_two_hbm, local_sem.at[4]),
    ]
    for store in stores:
        store.start()
    store_pred.wait()
    for store in stores:
        store.wait()


def local(n, state_in, target, ocean_mask, kernel_one, kernel_two):
    height, width, ch = state_in.shape
    cells, wide = height * width, 3 * ch
    ext = (height + 2) * width
    pad = padded_rows(n, wide)
    steps = n.bit_length() - 1
    deep = -(-(cells + width) // 128) * 128
    vmem, anywhere = pl.BlockSpec(memory_space=pltpu.VMEM), pl.BlockSpec(memory_space=pl.ANY)
    dma = pltpu.SemaphoreType.DMA
    prediction, grad_one, grad_two = pl.pallas_call(
        functools.partial(kernel, n, height, width, ch),
        out_shape=(
            jax.ShapeDtypeStruct((cells, ch), BF16),
            jax.ShapeDtypeStruct((3, pad, ch), BF16),
            jax.ShapeDtypeStruct((3, pad, ch), BF16),
        ),
        in_specs=[vmem, vmem, anywhere, anywhere, anywhere],
        out_specs=(anywhere, anywhere, anywhere),
        scratch_shapes=[
            pltpu.VMEM((cells, ch // 2), BF16),
            pltpu.VMEM((cells, ch), BF16),
            pltpu.VMEM((3, wide, ch), BF16),
            pltpu.VMEM((3, wide, ch), BF16),
            pltpu.VMEM((3, wide, ch), BF16),
            pltpu.VMEM((cells, ch), BF16),
            pltpu.VMEM((ext, wide), BF16),
            pltpu.VMEM((ext, wide), BF16),
            pltpu.VMEM((ext, wide), BF16),
            pltpu.VMEM((width, wide), BF16),
            pltpu.VMEM((wide, deep), BF16),
            pltpu.VMEM((wide, deep), BF16),
            pltpu.VMEM((cells, ch), F32),
            pltpu.VMEM((ext, ch), BF16),
            pltpu.VMEM((3, height, ch), F32),
            pltpu.VMEM((3, height, ch), F32),
            pltpu.VMEM((3, width, ch), F32),
            pltpu.VMEM((3, height, ch), F32),
            pltpu.VMEM((3, height, ch), F32),
            pltpu.VMEM((3, width, ch), F32),
            pltpu.VMEM((3, 8, ch), F32),
            pltpu.VMEM((3, 8, ch), F32),
            pltpu.VMEM((2, 3, pad, ch), F32),
            pltpu.VMEM((2, 3, 2, pad, ch // 2), BF16),
            pltpu.VMEM((2, 3, 2, pad, ch // 2), BF16),
            pltpu.VMEM((2, 3, pad, ch), BF16),
            dma((4, 5)),
            dma((4, 5)),
            dma((2, 3, 2 * steps, 2)),
            dma((2, 3, 2 * steps, 2)),
            dma((6,)),
        ],
        compiler_params=pltpu.CompilerParams(
            collective_id=0, has_side_effects=True, vmem_limit_bytes=60 * 1024 * 1024
        ),
        cost_estimate=pl.CostEstimate(
            flops=10 * cells * 9 * ch * ch, bytes_accessed=16 * cells * ch, transcendentals=2 * cells * ch
        ),
    )(
        state_in.reshape(cells, ch),
        ocean_mask,
        kernel_one.reshape(3, wide, ch),
        target.reshape(cells, ch),
        kernel_two.reshape(3, wide, ch),
    )
    shape = (3, 3, ch, ch)
    return (
        prediction.reshape(height, width, ch),
        grad_one[:, :wide].astype(F32).reshape(shape),
        grad_two[:, :wide].astype(F32).reshape(shape),
    )


def solution(mesh):
    return jax.shard_map(
        functools.partial(local, mesh.shape["lon"]),
        mesh=mesh,
        in_specs=(P("groups", "lon", None), P("groups", "lon", None), P("groups", "lon"), P(), P()),
        out_specs=(
            P("groups", "lon", None),
            P("groups", None, None, None),
            P("groups", None, None, None),
        ),
        check_vma=False,
    )
```

time: 107 us -> 94.3 us (0.88)
  Pallas kernels: 98 us -> 85.8 us
    pallas_call x1, Pallas kernels: 98 us -> 85.8 us  [local(): pl.pallas_call(functools.partial(kernel, n, height, width, ch), out_shape...]
    broadcast_in_dim x2 -> x0, local copies, waits for them, and re-layouts: 1.46 us -> none  [local(): jnp.broadcast_to(ocean_mask.astype(BF16)[..., None], (height, width, ch /...]
    unnamed x5 -> x6, local copies, waits for them, and re-layouts: 1.52 us -> 2.96 us
where the time goes in v2:
time: 94.3 us; the launch traced here: 94 us
  Pallas kernels  85.8 us (91%)
  other arithmetic  4.62 us (5%)
  local copies, waits for them, and re-layouts  2.96 us (3%)
    pallas_call x1, Pallas kernels, local(): pl.pallas_call(functools.partial(kernel, n, height, width, ch), out_shape...  85.8 us
    reshape x1, other arithmetic, local(): grad_one[:, :wide].astype(F32).reshape(shape)  2.99 us
    unnamed x6, local copies, waits for them, and re-layouts  2.96 us

profile of v2, /device:TPU:0, one launch (start us, length us, event | category | flops | bytes accessed | tf_op | source)
XLA Modules:
  0.0 94.0 jit_solution(6480428842981119131)
XLA Ops:
  0.6 1.4 %copy.8.ocean = s32[64,48]{1,0:T(8,128)} copy(s32[64,48]{0,1:T(8,128)} %param.7) | data formatting | bytes 24576 | tf_op args[2]
  2.1 85.8 %shard_map.76 = (bf16[3072,256]{1,0:T(8,128)(2,1)}, bf16[3,768,256]{2,1,0:T(8,128)(2,1)}, bf16[3,768,256]{2,1,0:T(8,128)(2,1)}) custom-call(bf16[3072,256]{1,0:T(8,128)(2,1)} %bitcast.12, s32[64,48]{1,0:T(8,128)} %copy.8.ocean, bf16[3,768,256]{2,1,0:T(8,128)(2,1)} %bitcast.14, bf16[3072,256]{1,0:T(8,128)(2,1)} %bitcast.13, bf16[3,768,256]{2,1,0:T(8,128)(2,1)} %bitcast.15), custom_call_target="tpu_custom_call" | custom-call | flops 18119393280 | bytes 12582912 | tf_op jit(solution)/shard_map/pallas_call | solution.py:397
  87.9 0.0 copy-start.1
  87.9 3.0 %convert.2 = f32[3,3,256,256]{3,2,1,0:T(8,128)} convert(bf16[3,3,256,256]{3,2,1,0:T(8,128)(2,1)} %bitcast.11) | non-fusion elementwise | flops 589824 | bytes 3538944 | tf_op jit(solution)/shard_map/reshape | solution.py:455
  90.9 0.0 copy-done.1
  90.9 0.0 copy-start
  90.9 1.6 %convert.3 = f32[3,3,256,256]{3,2,1,0:T(8,128)} convert(bf16[3,3,256,256]{3,2,1,0:T(8,128)(2,1)S(1)} %bitcast.10) | non-fusion elementwise | flops 589824 | bytes 3538944 | tf_op jit(solution)/shard_map/reshape | solution.py:456
  92.5 0.4 copy-done
  92.9 1.1 %copy.10 = bf16[64,48,256]{2,1,0:T(8,128)(2,1)} copy(bf16[64,48,256]{2,1,0:T(8,128)(2,1)S(1)} %bitcast.9) | data formatting | bytes 3145728
Async XLA Ops:
  87.9 3.0 %copy-start.1 = (bf16[3,768,256]{2,1,0:T(8,128)(2,1)S(1)}, bf16[3,768,256]{2,1,0:T(8,128)(2,1)}, u32[]{:S(2)}) copy-start(bf16[3,768,256]{2,1,0:T(8,128)(2,1)} %get-tuple-element.8) | copy-start | bytes 3538948
  90.9 2.0 %copy-start = (bf16[3072,256]{1,0:T(8,128)(2,1)S(1)}, bf16[3072,256]{1,0:T(8,128)(2,1)}, u32[]{:S(2)}) copy-start(bf16[3072,256]{1,0:T(8,128)(2,1)} %get-tuple-element.6) | copy-start | bytes 4718596

commit v3 on v2

--- a/solution.py
+++ b/solution.py
@@ -18,9 +18,14 @@
     return -(-total // unit) * unit
 
 
-def bit_orders(count):
-    bits = list(range(count.bit_length() - 1))
-    return bits, bits[:1] + bits[2:] + bits[1:2]
+def stage_list(count, far_first):
+    bits = count.bit_length() - 1
+    radices = [2] * (bits - 2) + [4] if bits >= 3 else [2] * bits
+    stages, stride = [], 1
+    for radix in radices:
+        stages.append((radix, stride))
+        stride *= radix
+    return stages[:1] + stages[:0:-1] if far_first else stages
 
 
 def kernel(
@@ -31,7 +36,7 @@
     x3, h3, e3, n3, xt, ht, slope, back,
     send_w, send_e, send_n, got_w, got_e, got_n, got_cw, got_ce,
     total, staged, landed, full,
-    halo_send, halo_recv, sum_send, sum_recv, local_sem,
+    halo_send, halo_recv, sum_send, sum_recv, local_sem, store_sem,
 ):
     me = lax.axis_index("lon")
     cells = height * width
@@ -41,8 +46,6 @@
     north_at = (height + 1) * width
     pad = total.shape[2]
     half = ch // 2
-    orders = bit_orders(n)
-    steps = len(orders[0])
 
     barrier = pltpu.get_barrier_semaphore()
     for k in range(1, n):
@@ -279,63 +282,64 @@
             field_t[:, 0:depth], error[at : at + depth, lanes], preferred_element_type=F32
         )
 
-    def partner(h, s):
-        bit = 1 << orders[h][s]
-        mine = lax.rem(me // bit, 2)
-        return mine, me + (1 - 2 * mine) * bit
-
     def sum_stages(g, p):
-        starts = [0, 0]
-        lanes = [slice(h * half, (h + 1) * half) for h in range(2)]
-        for s in range(steps):
-            size = pad >> (s + 1)
-            offset = pad - (pad >> s)
+        stages = stage_list(n, g == 1 and p == 0)
+        start, size, offset = 0, pad, 0
+        others = []
+        for s, (radix, stride) in enumerate(stages):
+            digit = lax.rem(me // stride, radix)
+            size //= radix
             flying = []
-            for h in range(2):
-                mine, to = partner(h, s)
-                away = pl.multiple_of(starts[h] + (1 - mine) * size, 16)
-                staged[g, p, h, offset : offset + size, :] = total[
-                    g, p, pl.ds(away, size), lanes[h]
-                ].astype(BF16)
+            for o in range(1, radix):
+                j = lax.rem(digit + o, radix)
+                away = pl.multiple_of(start + j * size, 16)
+                spot = pl.ds(offset + (o - 1) * size, size)
+                staged[g, p, spot, :] = total[g, p, pl.ds(away, size), :].astype(BF16)
                 copy = pltpu.make_async_remote_copy(
-                    src_ref=staged.at[g, p, h, pl.ds(offset, size)],
-                    dst_ref=landed.at[g, p, h, pl.ds(offset, size)],
-                    send_sem=sum_send.at[g, p, s, h], recv_sem=sum_recv.at[g, p, s, h],
-                    device_id={"lon": to}, device_id_type=MESH,
+                    src_ref=staged.at[g, p, spot], dst_ref=landed.at[g, p, spot],
+                    send_sem=sum_send.at[g, p, s, o - 1], recv_sem=sum_recv.at[g, p, s, o - 1],
+                    device_id={"lon": me + (j - digit) * stride}, device_id_type=MESH,
+                )
+                copy.start()
+                flying.append((copy, spot))
+            start = start + digit * size
+            yield
+            at = pl.ds(pl.multiple_of(start, 16), size)
+            own = total[g, p, at, :]
+            for copy, spot in flying:
+                copy.wait()
+                own = own + landed[g, p, spot, :].astype(F32)
+            if s + 1 < len(stages):
+                total[g, p, at, :] = own
+            else:
+                full[g, p, at, :] = own.astype(BF16)
+            offset += (radix - 1) * size
+        for s, (radix, stride) in reversed(list(enumerate(stages))):
+            digit = lax.rem(me // stride, radix)
+            slot = 2 * len(stages) - 1 - s
+            own = full.at[g, p, pl.ds(pl.multiple_of(start, 16), size)]
+            flying = []
+            for o in range(1, radix):
+                j = lax.rem(digit + o, radix)
+                copy = pltpu.make_async_remote_copy(
+                    src_ref=own, dst_ref=own,
+                    send_sem=sum_send.at[g, p, slot, o - 1], recv_sem=sum_recv.at[g, p, slot, o - 1],
+                    device_id={"lon": me + (j - digit) * stride}, device_id_type=MESH,
                 )
                 copy.start()
                 flying.append(copy)
-                starts[h] = starts[h] + mine * size
-            yield
-            for h in range(2):
-                flying[h].wait()
-                at = pl.ds(pl.multiple_of(starts[h], 16), size)
-                total[g, p, at, lanes[h]] = total[g, p, at, lanes[h]] + landed[
-                    g, p, h, offset : offset + size, :
-                ].astype(F32)
-        for h in range(2):
-            at = pl.ds(pl.multiple_of(starts[h], 16), pad >> steps)
-            full[g, p, at, lanes[h]] = total[g, p, at, lanes[h]].astype(BF16)
-        for s in reversed(range(steps)):
-            size = pad >> (s + 1)
-            slot = 2 * steps - 1 - s
-            flying = []
-            for h in range(2):
-                mine, to = partner(h, s)
-                at = pl.ds(pl.multiple_of(starts[h], 16), size)
-                own = full.at[g, p, at, pl.ds(h * half, half)]
-                copy = pltpu.make_async_remote_copy(
-                    src_ref=own, dst_ref=own,
-                    send_sem=sum_send.at[g, p, slot, h], recv_sem=sum_recv.at[g, p, slot, h],
-                    device_id={"lon": to}, device_id_type=MESH,
-                )
-                copy.start()
-                flying.append(copy)
-                starts[h] = starts[h] - mine * size
+            start = start - digit * size
+            size *= radix
             yield
             for copy in flying:
                 copy.wait()
-
+        store = pltpu.make_async_copy(
+            full.at[g, p], (grad_two_hbm if g else grad_one_hbm).at[p], store_sem.at[g, p]
+        )
+        store.start()
+        stores.append(store)
+
+    stores = []
     sums = []
 
     def advance():
@@ -374,12 +378,6 @@
         advance()
     while sums:
         advance()
-    stores = [
-        pltpu.make_async_copy(full.at[0], grad_one_hbm, local_sem.at[3]),
-        pltpu.make_async_copy(full.at[1], grad_two_hbm, local_sem.at[4]),
-    ]
-    for store in stores:
-        store.start()
     store_pred.wait()
     for store in stores:
         store.wait()
@@ -390,7 +388,7 @@
     cells, wide = height * width, 3 * ch
     ext = (height + 2) * width
     pad = padded_rows(n, wide)
-    steps = n.bit_length() - 1
+    steps = len(stage_list(n, False))
     deep = -(-(cells + width) // 128) * 128
     vmem, anywhere = pl.BlockSpec(memory_space=pltpu.VMEM), pl.BlockSpec(memory_space=pl.ANY)
     dma = pltpu.SemaphoreType.DMA
@@ -427,14 +425,15 @@
             pltpu.VMEM((3, 8, ch), F32),
             pltpu.VMEM((3, 8, ch), F32),
             pltpu.VMEM((2, 3, pad, ch), F32),
-            pltpu.VMEM((2, 3, 2, pad, ch // 2), BF16),
-            pltpu.VMEM((2, 3, 2, pad, ch // 2), BF16),
+            pltpu.VMEM((2, 3, pad, ch), BF16),
+            pltpu.VMEM((2, 3, pad, ch), BF16),
             pltpu.VMEM((2, 3, pad, ch), BF16),
             dma((4, 5)),
             dma((4, 5)),
-            dma((2, 3, 2 * steps, 2)),
-            dma((2, 3, 2 * steps, 2)),
+            dma((2, 3, 2 * steps, 3)),
+            dma((2, 3, 2 * steps, 3)),
             dma((6,)),
+            dma((2, 3)),
         ],
         compiler_params=pltpu.CompilerParams(
             collective_id=0, has_side_effects=True, vmem_limit_bytes=60 * 1024 * 1024

time: 94.3 us -> 102 us (1.082)
  Pallas kernels: 85.8 us -> 93.3 us
    pallas_call x1, Pallas kernels: 85.8 us -> 93.3 us  [local(): pl.pallas_call(functools.partial(kernel, n, height, width, ch), out_shape...]
where the time goes in v3:
time: 102 us
  Pallas kernels  93.3 us (91%)
  other arithmetic  4.62 us (5%)
  local copies, waits for them, and re-layouts  2.96 us (3%)
    pallas_call x1, Pallas kernels, local(): pl.pallas_call(functools.partial(kernel, n, height, width, ch), out_shape...  93.3 us
    reshape x1, other arithmetic, local(): grad_one[:, :wide].astype(F32).reshape(shape)  2.99 us
    unnamed x6, local copies, waits for them, and re-layouts  2.96 us

profile of v3, /device:TPU:0, one launch (start us, length us, event | category | flops | bytes accessed | tf_op | source)
XLA Modules:
  0.0 101.5 jit_solution(883280556276295346)
XLA Ops:
  0.6 1.4 %copy.8.ocean = s32[64,48]{1,0:T(8,128)} copy(s32[64,48]{0,1:T(8,128)} %param.7) | data formatting | bytes 24576 | tf_op args[2]
  2.1 93.3 %shard_map.76 = (bf16[3072,256]{1,0:T(8,128)(2,1)}, bf16[3,768,256]{2,1,0:T(8,128)(2,1)}, bf16[3,768,256]{2,1,0:T(8,128)(2,1)}) custom-call(bf16[3072,256]{1,0:T(8,128)(2,1)} %bitcast.12, s32[64,48]{1,0:T(8,128)} %copy.8.ocean, bf16[3,768,256]{2,1,0:T(8,128)(2,1)} %bitcast.14, bf16[3072,256]{1,0:T(8,128)(2,1)} %bitcast.13, bf16[3,768,256]{2,1,0:T(8,128)(2,1)} %bitcast.15), custom_call_target="tpu_custom_call" | custom-call | flops 18119393280 | bytes 12582912 | tf_op jit(solution)/shard_map/pallas_call | solution.py:395
  95.4 0.0 copy-start.1
  95.4 3.0 %convert.2 = f32[3,3,256,256]{3,2,1,0:T(8,128)} convert(bf16[3,3,256,256]{3,2,1,0:T(8,128)(2,1)} %bitcast.11) | non-fusion elementwise | flops 589824 | bytes 3538944 | tf_op jit(solution)/shard_map/reshape | solution.py:454
  98.4 0.0 copy-done.1
  98.4 0.0 copy-start
  98.4 1.6 %convert.3 = f32[3,3,256,256]{3,2,1,0:T(8,128)} convert(bf16[3,3,256,256]{3,2,1,0:T(8,128)(2,1)S(1)} %bitcast.10) | non-fusion elementwise | flops 589824 | bytes 3538944 | tf_op jit(solution)/shard_map/reshape | solution.py:455
  100.0 0.4 copy-done
  100.4 1.1 %copy.10 = bf16[64,48,256]{2,1,0:T(8,128)(2,1)} copy(bf16[64,48,256]{2,1,0:T(8,128)(2,1)S(1)} %bitcast.9) | data formatting | bytes 3145728
Async XLA Ops:
  95.4 3.0 %copy-start.1 = (bf16[3,768,256]{2,1,0:T(8,128)(2,1)S(1)}, bf16[3,768,256]{2,1,0:T(8,128)(2,1)}, u32[]{:S(2)}) copy-start(bf16[3,768,256]{2,1,0:T(8,128)(2,1)} %get-tuple-element.8) | copy-start | bytes 3538948
  98.4 2.0 %copy-start = (bf16[3072,256]{1,0:T(8,128)(2,1)S(1)}, bf16[3072,256]{1,0:T(8,128)(2,1)}, u32[]{:S(2)}) copy-start(bf16[3072,256]{1,0:T(8,128)(2,1)} %get-tuple-element.6) | copy-start | bytes 4718596
